TPU v7x, 32 devices: a whole 2x2x4 slice. The times are simulated.
32 devices in a mesh: blk: 4 (over x, core), grp: 8 (over z, y).
Axes of the slice: x: 2, y: 2, z: 4, core: 2. Of those that a mesh axis runs over, the one named last changes fastest.
Arguments:
- amplitudes: bfloat16 [8192, 512], P('grp', 'blk'), may hold values from -6 to 6
- amp_tiles: int32 [64, 4], P('grp', 'blk'), may hold values from 0 to 1
- cd_width: int32 [4], P('blk'), may hold values from 64 to 128
- integrals: bfloat16 [8, 128, 4096], P('grp', None, 'blk'), may hold values from -0.25 to 0.25
- int_tiles: int32 [8, 32], P('grp', 'blk'), may hold values 0 or 1
- ab_width: int32 [32], P('blk'), may hold values from 64 to 128
- owners: int32 [4], replicated, may hold values from 0 to 7, as said below
Outputs:
- ladder: bfloat16 [8192, 4096], P('grp', 'blk')
Inputs may be any that keep to these rules, and one draw needn't show every extreme that they name: `owners`: the 4 entries are distinct owner slots.
All inputs are finite; a program needn't handle non-finite values. No bound on the sum of `int_tiles` on one device may be relied on, other than what follows from the above.
Results may differ from a plain program's by a relative error of at most 0.001.
Values may be sent and summed in bfloat16 or wider, within the bound.
A program may use at most 64 MiB of HBM per device.

v0:
```python
import jax
import jax.numpy as jnp
from jax import lax
from jax.sharding import PartitionSpec as P


def from_root(x, axis, root):
    mine = lax.axis_index(axis) == root
    return lax.psum(jnp.where(mine, x, jnp.zeros_like(x)), axis)


def from_behind(value, axis, steps):
    count = lax.axis_size(axis)
    pairs = [(source, (source + steps) % count) for source in range(count)]
    return lax.ppermute(value, axis, pairs)


def per_device(amplitudes, amp_tiles, cd_width, integrals, int_tiles, ab_width, owners):
    row_count, tile_size = amplitudes.shape
    tile_rows = row_count // tile_size
    ab_local = int_tiles.shape[1]
    panel_width = ab_local * tile_size
    blocks = lax.axis_size("blk")
    my_block = lax.axis_index("blk")
    within_tile = jnp.arange(tile_size)
    zero_value = jnp.zeros((), jnp.bfloat16)
    keep_amp = (amp_tiles[:, :, None] > 0) & (within_tile[None, None, :] < cd_width[0])
    masked_amps = jnp.where(
        keep_amp, amplitudes.reshape(tile_rows, tile_size, tile_size), zero_value
    )
    masked_amps = masked_amps.reshape(row_count, tile_size)
    tiled_ints = integrals.reshape(tile_size, ab_local, tile_size)
    own_panel = jnp.where(int_tiles[0][None, :, None] > 0, tiled_ints, zero_value).reshape(
        tile_size, panel_width
    )
    panel_list = []
    for tile_idx in range(blocks):
        panel_list.append(from_root(own_panel, "grp", owners[tile_idx]))
    stacked = jnp.stack(panel_list)
    running = jnp.zeros((row_count, panel_width), jnp.float32)
    current = masked_amps
    for step_idx in range(blocks):
        source_idx = (my_block + -step_idx) % blocks
        running = running + jnp.dot(
            current,
            lax.dynamic_index_in_dim(stacked, source_idx, 0, keepdims=False),
            preferred_element_type=jnp.float32,
        )
        if step_idx + 1 < blocks:
            current = from_behind(current, "blk", 1)
    column_keep = (within_tile[None, :] < ab_width[:, None]).reshape(panel_width)
    return jnp.where(column_keep[None, :], 0.5 * running, 0.0).astype(jnp.bfloat16)


def solution(mesh):
    placed = (
        P("grp", "blk"),
        P("grp", "blk"),
        P("blk"),
        P("grp", None, "blk"),
        P("grp", "blk"),
        P("blk"),
        P(),
    )
    return jax.shard_map(
        per_device, mesh=mesh, in_specs=placed, out_specs=P("grp", "blk"), check_vma=False
    )
```

profile of v0, /device:TPU:0, one launch (start us, length us, event | category | flops | bytes accessed | tf_op | source)
XLA Modules:
  0.0 110.3 jit_solution(10149197401938779249)
XLA Ops:
  6.5 0.7 compare_bitcast_fusion
  7.2 0.1 broadcast_bitcast_fusion
  7.3 1.5 %fusion.16 = (s32[1]{0:T(128)}, s32[1]{0:T(128)}, s32[1]{0:T(128)}, s32[1]{0:T(128)}) fusion(s32[4]{0:T(128)} %param.13), kind=kLoop, calls=%fused_computation.33 | loop fusion | bytes 32 | tf_op jit(solution)/shard_map/slice | solution.py:38
  11.3 1.9 %select_bitcast_fusion = (bf16[1,128,1024]{2,1,0:T(8,128)(2,1)}, bf16[1,128,1024]{2,1,0:T(8,128)(2,1)}, bf16[1,128,1024]{2,1,0:T(8,128)(2,1)}, bf16[1,128,1024]{2,1,0:T(8,128)(2,1)}) fusion(pred[]{:T(512)S(6)} %eq.20, bf16[1,128,1024]{2,1,0:T(8,128)(2,1)} %param.10, pred[1024]{0:T(1024)(128)(4,1)S(1)} %broadcast_bitcast_fusion, pred[]{:T(512)S(6)} %eq.18, ...), kind=kLoop, calls=%fused_computation.14 | loop fusion | flops 655360 | bytes 1311748 | tf_op jit(solution)/shard_map/stack | solution.py:39
  13.2 0.0 all-reduce.3.cloned.1.call-update
  13.9 0.7 compare_bitcast_fusion.1
  14.5 0.1 broadcast_and_fusion
  14.6 1.0 bitcast_select_fusion
  15.6 0.5 collective-permute-start
  16.1 6.0 %collective-permute-done = bf16[1024,128]{1,0:T(8,128)(2,1)S(1)} collective-permute-done((bf16[1024,128]{1,0:T(8,128)(2,1)S(1)}, bf16[1024,128]{1,0:T(8,128)(2,1)S(1)}, u32[]{:S(2)}, u32[]{:S(2)}) %collective-permute-start) | collective-permute-done | bytes 262176 | tf_op jit(solution)/shard_map/ppermute | solution.py:15
  22.1 0.0 collective-permute-start.1
  22.1 0.7 fusion.11
  22.8 5.1 %collective-permute-done.1 = bf16[1024,128]{1,0:T(8,128)(2,1)S(1)} collective-permute-done((bf16[1024,128]{1,0:T(8,128)(2,1)S(1)}, bf16[1024,128]{1,0:T(8,128)(2,1)S(1)}, u32[]{:S(2)}, u32[]{:S(2)}) %collective-permute-start.1) | collective-permute-done | bytes 262176 | tf_op jit(solution)/shard_map/ppermute | solution.py:15
  27.9 0.0 collective-permute-start.2
  27.9 67.2 %all-reduce.3.cloned.1.call-done = (bf16[1,128,1024]{2,1,0:T(8,128)(2,1)}, bf16[1,128,1024]{2,1,0:T(8,128)(2,1)}, bf16[1,128,1024]{2,1,0:T(8,128)(2,1)}, bf16[1,128,1024]{2,1,0:T(8,128)(2,1)}) async-done(((bf16[1,128,1024]{2,1,0:T(8,128)(2,1)}, bf16[1,128,1024]{2,1,0:T(8,128)(2,1)}, bf16[1,128,1024]{2,1,0:T(8,128)(2,1)}, bf16[1,128,1024]{2,1,0:T(8,128)(2,1)}), (bf16[1,128,1024]{2,1,0:T(8,128)(2,1)}, ...) | async-done | bytes 1048592 | tf_op jit(solution)/shard_map/psum | solution.py:9
  95.1 1.0 constant_dynamic-update-slice_fusion.3
  96.1 1.0 constant_dynamic-update-slice_fusion.2
  97.0 1.0 constant_dynamic-update-slice_fusion.1
  98.0 1.0 constant_dynamic-update-slice_fusion
  99.0 0.7 fusion.5
  99.7 0.7 fusion.1
  100.4 0.7 fusion.3
  101.1 0.0 collective-permute-done.2
  101.1 2.4 %select_convert_fusion = bf16[1024,1024]{1,0:T(8,128)(2,1)} fusion(f32[1024,1024]{1,0:T(8,128)S(1)} %fusion.1, f32[1024,1024]{1,0:T(8,128)S(1)} %fusion.5, f32[1024,1024]{1,0:T(8,128)S(1)} %fusion.3, bf16[1024,128]{1,0:T(8,128)(2,1)S(1)} %collective-permute-done.2, pred[1024]{0:T(1024)(128)(4,1)S(1)} %fusion.11, ...), kind=kOutput, calls=%fused_computation | convolution fusion | flops 274726912 | bytes 15205380 | tf_op jit(solution)/shard_map/dot_general | solution.py:44
  (2 shorter events, 0.0 us)
Async XLA Ops:
  6.5 88.5 %all-reduce.3.cloned.1.call-start = ((), (), s32[]{:S(2)}) async-start(), calls=%async_computation | async-start | bytes 2097152 | tf_op jit(solution)/shard_map/psum | solution.py:9
  15.6 6.5 %collective-permute-start = (bf16[1024,128]{1,0:T(8,128)(2,1)S(1)}, bf16[1024,128]{1,0:T(8,128)(2,1)S(1)}, u32[]{:S(2)}, u32[]{:S(2)}) collective-permute-start(bf16[1024,128]{1,0:T(8,128)(2,1)S(1)} %bitcast_select_fusion), channel_id=1, source_target_pairs={{0,8},{8,16},{16,24},{24,0},{1,9},{9,17},{17,25},{25,1},{2,10},{10... | collective-permute-start | bytes 786440 | tf_op jit(solution)/shard_map/ppermute | solution.py:15
  22.1 5.8 %collective-permute-start.1 = (bf16[1024,128]{1,0:T(8,128)(2,1)S(1)}, bf16[1024,128]{1,0:T(8,128)(2,1)S(1)}, u32[]{:S(2)}, u32[]{:S(2)}) collective-permute-start(bf16[1024,128]{1,0:T(8,128)(2,1)S(1)} %collective-permute-done), channel_id=1, source_target_pairs={{0,8},{8,16},{16,24},{24,0},{1,9},{9,17},{17,25},{25,1},{2,10},{10... | collective-permute-start | bytes 786440 | tf_op jit(solution)/shard_map/ppermute | solution.py:15
  27.9 73.2 %collective-permute-start.2 = (bf16[1024,128]{1,0:T(8,128)(2,1)S(1)}, bf16[1024,128]{1,0:T(8,128)(2,1)S(1)}, u32[]{:S(2)}, u32[]{:S(2)}) collective-permute-start(bf16[1024,128]{1,0:T(8,128)(2,1)S(1)} %collective-permute-done.1), channel_id=1, source_target_pairs={{0,8},{8,16},{16,24},{24,0},{1,9},{9,17},{17,25},{25,1},{2,10},{10... | collective-permute-start | bytes 786440 | tf_op jit(solution)/shard_map/ppermute | solution.py:15
Sparse Core Ops, SparseCore 0:
  13.3 81.7 all-reduce.2
where the time goes:
time: 111 us; the launch traced here: 110 us
  waiting for transfers between devices  78.3 us (71%)
  between operations  16.6 us (15%)
  local copies, waits for them, and re-layouts  5.41 us (5%)
  other arithmetic  5.03 us (5%)
  matrix products  4.49 us (4%)
    psum x1, waiting for transfers between devices, from_root(): return lax.psum(jnp.where(mine, x, jnp.zeros_like(x)), axis)  67.2 us
    ppermute x3, waiting for transfers between devices, from_behind(): return lax.ppermute(value, axis, pairs)  11.1 us
    dot_general x4, matrix products, per_device(): jnp.dot(current, lax.dynamic_index_in_dim(stacked, source_idx, 0, keepdim...  4.49 us
    unnamed x3, local copies, waits for them, and re-layouts  2.9 us
  transfers between devices with their start and end apart: 4, of which 3 were waited for; matrix products, arithmetic and copies ran while one was open for 8% of the time, Pallas kernels for 0%

commit v1 on v0

v1 whole, which is shorter than its diff:
```python
import functools

import jax
import jax.numpy as jnp
from jax import lax
from jax.experimental import pallas as pl
from jax.experimental.pallas import tpu as pltpu
from jax.sharding import PartitionSpec as P

UP, DOWN, PAIR = 0, 1, 2


class Gather:
    def __init__(self, axis, count, own, slot_of, send_sem, recv_sem):
        me = lax.axis_index(axis)
        self.axis, self.half = axis, count // 2
        self.pos, self.side = me // 2, me % 2
        self.own, self.slot_of = own, slot_of
        self.send_sem, self.recv_sem = send_sem, recv_sem
        self.not_last = self.pos + 1 < self.half
        self.not_first = self.pos > 0
        self.up = {axis: jnp.minimum(self.pos + 1, self.half - 1) * 2 + self.side}
        self.down = {axis: jnp.maximum(self.pos - 1, 0) * 2 + self.side}
        self.pair = {axis: self.pos * 2 + 1 - self.side}

    def signal_all(self, barrier):
        def to(device):
            pl.semaphore_signal(
                barrier, inc=1, device_id=device, device_id_type=pl.DeviceIdType.MESH
            )

        to(self.pair)
        pl.when(self.not_last)(lambda: to(self.up))
        pl.when(self.not_first)(lambda: to(self.down))

    def neighbours(self):
        return 1 + self.not_last.astype(jnp.int32) + self.not_first.astype(jnp.int32)

    def copy(self, kind, p, src=None, side=None):
        slot = self.slot_of(p * 2 + (self.side if side is None else side))
        return pltpu.make_async_remote_copy(
            src_ref=slot if src is None else src,
            dst_ref=slot,
            send_sem=self.send_sem.at[kind, p],
            recv_sem=self.recv_sem.at[kind, p],
            device_id=(self.up, self.down, self.pair)[kind],
            device_id_type=pl.DeviceIdType.MESH,
        )

    def begin(self):
        pl.when(self.not_last)(lambda: self.copy(UP, self.pos, self.own).start())
        pl.when(self.not_first)(lambda: self.copy(DOWN, self.pos, self.own).start())
        self.copy(PAIR, self.pos, self.own).start()

    def steps(self, first, last):
        def step(s, carry):
            below, above = self.pos - 1 - s, self.pos + 1 + s

            @pl.when(below >= 0)
            def _():
                self.copy(UP, below).wait_recv()
                pl.when(self.not_last)(lambda: self.copy(UP, below).start())
                self.copy(PAIR, below).start()

            @pl.when(above < self.half)
            def _():
                self.copy(DOWN, above).wait_recv()
                pl.when(self.not_first)(lambda: self.copy(DOWN, above).start())
                self.copy(PAIR, above).start()

            return carry

        lax.fori_loop(first, last, step, 0)

    def finish(self):
        def one(p, carry):
            self.copy(PAIR, p, side=1 - self.side).wait_recv()
            self.copy(PAIR, p).wait_send()

            @pl.when(self.not_last & (p <= self.pos))
            def _():
                self.copy(UP, p).wait_send()

            @pl.when(self.not_first & (p >= self.pos))
            def _():
                self.copy(DOWN, p).wait_send()

            return carry

        lax.fori_loop(0, self.half, one, 0)


def gather_kernel(
    groups, blocks, amps, amp_tiles, cd_width, ints, int_tiles,
    panels_out, amps_out, own_panel, own_amps, panel_send, panel_recv, amp_send, amp_recv, local,
):
    rows, tile = amps.shape
    width = ints.shape[2]
    panels = Gather("grp", groups, own_panel, lambda i: panels_out.at[i], panel_send, panel_recv)
    amplitudes = Gather(
        "blk", blocks, own_amps,
        lambda i: amps_out.at[:, pl.ds(pl.multiple_of(i * tile, tile), tile)],
        amp_send, amp_recv,
    )
    barrier = pltpu.get_barrier_semaphore()
    panels.signal_all(barrier)
    amplitudes.signal_all(barrier)

    for j in range(width // tile):
        cols = slice(j * tile, (j + 1) * tile)
        keep = jnp.full((tile, tile), int_tiles[0, j], jnp.int32) > 0
        own_panel[:, cols] = jnp.where(keep, ints[0, :, cols].astype(jnp.float32), 0.0).astype(
            jnp.bfloat16
        )
    pl.semaphore_wait(barrier, panels.neighbours() + amplitudes.neighbours())
    panels.begin()

    within = lax.broadcasted_iota(jnp.int32, (tile, tile), 1) < cd_width[0]
    for r in range(rows // tile):
        part = slice(r * tile, (r + 1) * tile)
        keep = (jnp.full((tile, tile), amp_tiles[r, 0], jnp.int32) > 0) & within
        own_amps[part, :] = jnp.where(keep, amps[part, :].astype(jnp.float32), 0.0).astype(
            jnp.bfloat16
        )
    amplitudes.begin()

    keep_panel = pltpu.make_async_copy(
        own_panel, panels_out.at[lax.axis_index("grp")], local.at[0]
    )
    keep_amps = pltpu.make_async_copy(
        own_amps, amplitudes.slot_of(lax.axis_index("blk")), local.at[1]
    )
    keep_panel.start()
    keep_amps.start()
    panels.steps(0, 1)
    amplitudes.steps(0, blocks // 2 - 1)
    panels.steps(1, groups // 2 - 1)
    amplitudes.finish()
    panels.finish()
    keep_panel.wait()
    keep_amps.wait()


def multiply_kernel(owners, ab_width, amps, panels, out, chosen, sem):
    tile = panels.shape[1]
    count = chosen.shape[0] // tile

    @pl.when(pl.program_id(0) == 0)
    def _():
        copies = [
            pltpu.make_async_copy(
                panels.at[owners[t]], chosen.at[pl.ds(t * tile, tile)], sem.at[t]
            )
            for t in range(count)
        ]
        for copy in copies:
            copy.start()
        for copy in copies:
            copy.wait()

    column = lax.broadcasted_iota(jnp.int32, (out.shape[0], 2 * tile), 1)
    for j in range(0, out.shape[1] // tile, 2):
        cols = slice(j * tile, (j + 2) * tile)
        total = jnp.dot(amps[...], chosen[:, cols], preferred_element_type=jnp.float32)
        limit = jnp.where(column < tile, ab_width[j], tile + ab_width[j + 1])
        out[:, cols] = jnp.where(column < limit, 0.5 * total, 0.0).astype(out.dtype)


def per_device(amplitudes, amp_tiles, cd_width, integrals, int_tiles, ab_width, owners):
    rows, tile = amplitudes.shape
    width = integrals.shape[2]
    groups, blocks = lax.axis_size("grp"), lax.axis_size("blk")
    vmem = pl.BlockSpec(memory_space=pltpu.VMEM)
    smem = pl.BlockSpec(memory_space=pltpu.SMEM)
    anywhere = pl.BlockSpec(memory_space=pl.ANY)
    panels, amps = pl.pallas_call(
        functools.partial(gather_kernel, groups, blocks),
        out_shape=(
            jax.ShapeDtypeStruct((groups, tile, width), jnp.bfloat16),
            jax.ShapeDtypeStruct((rows, blocks * tile), jnp.bfloat16),
        ),
        in_specs=[vmem, smem, smem, vmem, smem],
        out_specs=(anywhere, anywhere),
        scratch_shapes=[
            pltpu.VMEM((tile, width), jnp.bfloat16),
            pltpu.VMEM((rows, tile), jnp.bfloat16),
            pltpu.SemaphoreType.DMA((3, groups // 2)),
            pltpu.SemaphoreType.DMA((3, groups // 2)),
            pltpu.SemaphoreType.DMA((3, blocks // 2)),
            pltpu.SemaphoreType.DMA((3, blocks // 2)),
            pltpu.SemaphoreType.DMA((2,)),
        ],
        compiler_params=pltpu.CompilerParams(
            collective_id=0, has_side_effects=True, vmem_limit_bytes=16 * 2**20
        ),
    )(amplitudes, amp_tiles, cd_width, integrals, int_tiles)
    step = 256
    return pl.pallas_call(
        multiply_kernel,
        out_shape=jax.ShapeDtypeStruct((rows, width), jnp.bfloat16),
        grid=(rows // step,),
        in_specs=[smem, smem, pl.BlockSpec((step, blocks * tile), lambda i: (i, 0)), anywhere],
        out_specs=pl.BlockSpec((step, width), lambda i: (i, 0)),
        scratch_shapes=[
            pltpu.VMEM((blocks * tile, width), jnp.bfloat16),
            pltpu.SemaphoreType.DMA((blocks,)),
        ],
        compiler_params=pltpu.CompilerParams(vmem_limit_bytes=16 * 2**20),
    )(owners, ab_width, amps, panels)


def solution(mesh):
    placed = (
        P("grp", "blk"),
        P("grp", "blk"),
        P("blk"),
        P("grp", None, "blk"),
        P("grp", "blk"),
        P("blk"),
        P(),
    )
    return jax.shard_map(
        per_device, mesh=mesh, in_specs=placed, out_specs=P("grp", "blk"), check_vma=False
    )
```

time: 111 us -> 39.9 us (0.36)
  waiting for transfers between devices: 78.3 us -> 0 us
  Pallas kernels: 0 us -> 34.4 us
  between operations: 16.6 us -> 0.67 us
  other arithmetic: 5.03 us -> 0 us
  matrix products: 4.49 us -> 0 us
    psum x1 -> x0, waiting for transfers between devices: 67.2 us -> none  [from_root(): return lax.psum(jnp.where(mine, x, jnp.zeros_like(x)), axis)]
    pallas_call x0 -> x2, Pallas kernels: none -> 34.4 us  [the longest x1 30.8 us: per_device(): pl.pallas_call(functools.partial(gather_kernel, groups, blocks), out_shap...]
    ppermute x3 -> x0, waiting for transfers between devices: 11.1 us -> none  [from_behind(): return lax.ppermute(value, axis, pairs)]
    dot_general x4 -> x0, matrix products: 4.49 us -> none  [per_device(): jnp.dot(current, lax.dynamic_index_in_dim(stacked, source_idx, 0, keepdim...]
    another operation x1 -> x0, other arithmetic: 1.93 us -> none  [per_device(): stacked = jnp.stack(panel_list)]
    unnamed x3 -> x11, local copies, waits for them, and re-layouts: 2.9 us -> 4.59 us
    slice x1 -> x0, local copies, waits for them, and re-layouts: 1.46 us -> none  [per_device(): panel_list.append(from_root(own_panel, 'grp', owners[tile_idx]))]
    gt x2 -> x0, other arithmetic: 1.32 us -> none  [the longest x1 0.66 us: per_device(): amp_tiles[:, :, None] > 0]
  transfers between devices with their start and end apart: 4 -> 0, of which waited for: 3 -> 0; matrix products, arithmetic and copies ran while one was open for 8% -> 0% of each run, Pallas kernels for 0% -> 0%
where the time goes in v1:
time: 39.9 us; the launch traced here: 39.7 us
  Pallas kernels  34.4 us (86%)
  local copies, waits for them, and re-layouts  4.59 us (12%)
  between operations  0.67 us (2%)
    pallas_call x1, Pallas kernels, per_device(): pl.pallas_call(functools.partial(gather_kernel, groups, blocks), out_shap...  30.8 us
    unnamed x11, local copies, waits for them, and re-layouts  4.59 us
    pallas_call x1, Pallas kernels, per_device(): pl.pallas_call(multiply_kernel, out_shape=jax.ShapeDtypeStruct((rows, wid...  3.62 us

profile of v1, /device:TPU:0, one launch (start us, length us, event | category | flops | bytes accessed | tf_op | source)
XLA Modules:
  0.0 39.7 jit_solution(11497701355356959633)
XLA Ops:
  0.7 0.7 %copy.8.amp_tiles = s32[8,1]{1,0:T(8,128)S(1)} copy(s32[8,1]{0,1:T(1,128)} %param.8) | data formatting | bytes 64 | tf_op args[1]
  1.4 0.0 copy-start
  1.4 0.9 %copy-done = bf16[1024,128]{1,0:T(8,128)(2,1)S(1)} copy-done((bf16[1024,128]{1,0:T(8,128)(2,1)S(1)}, bf16[1024,128]{1,0:T(8,128)(2,1)}, u32[]{:S(2)}) %copy-start) | copy-done | bytes 262168
  2.3 0.0 copy-start.1
  2.3 0.9 %copy-done.1 = bf16[1,128,1024]{2,1,0:T(8,128)(2,1)S(1)} copy-done((bf16[1,128,1024]{2,1,0:T(8,128)(2,1)S(1)}, bf16[1,128,1024]{2,1,0:T(8,128)(2,1)}, u32[]{:S(2)}) %copy-start.1) | copy-done | bytes 262168
  3.3 0.0 copy-start.4
  3.3 0.7 %copy-done.4 = s32[1,8]{1,0:T(1,128)S(1)} copy-done((s32[1,8]{1,0:T(1,128)S(1)}, s32[1,8]{1,0:T(1,128)}, u32[]{:S(2)}) %copy-start.4) | copy-done | bytes 56
  3.9 30.8 %shard_map.73 = (bf16[8,128,1024]{2,1,0:T(8,128)(2,1)S(1)}, bf16[1024,512]{1,0:T(8,128)(2,1)S(1)}) custom-call(bf16[1024,128]{1,0:T(8,128)(2,1)S(1)} %copy-done, s32[8,1]{1,0:T(8,128)S(1)} %copy.8.amp_tiles, s32[1]{0:T(128)S(6)} %copy.9.cd_width, bf16[1,128,1024]{2,1,0:T(8,128)(2,1)S(1)} %copy-done.1, s32[1,8]{1,0:T(1,128)S(1)} %copy-done.4), custom_call_target="tpu_custom_call" | custom-call | tf_op jit(solution)/shard_map/pallas_call | solution.py:176
  34.7 0.0 copy-start.2
  34.7 0.6 %copy-done.2 = s32[4]{0:T(128)S(1)} copy-done((s32[4]{0:T(128)S(1)}, s32[4]{0:T(128)}, u32[]{:S(2)}) %copy-start.2) | copy-done | bytes 40
  35.4 0.0 copy-start.3
  35.4 0.7 %copy-done.3 = s32[8]{0:T(128)S(1)} copy-done((s32[8]{0:T(128)S(1)}, s32[8]{0:T(128)}, u32[]{:S(2)}) %copy-start.3) | copy-done | bytes 56
  36.0 3.6 %shard_map.74 = bf16[1024,1024]{1,0:T(8,128)(2,1)} custom-call(s32[4]{0:T(128)S(1)} %copy-done.2, s32[8]{0:T(128)S(1)} %copy-done.3, bf16[1024,512]{1,0:T(8,128)(2,1)S(1)} %get-tuple-element.7.amps, bf16[8,128,1024]{2,1,0:T(8,128)(2,1)S(1)} %get-tuple-element.8.panels), custom_call_target="tpu_custom_call" | custom-call | tf_op jit(solution)/shard_map/pallas_call | solution.py:198
Async XLA Ops:
  1.4 0.9 %copy-start = (bf16[1024,128]{1,0:T(8,128)(2,1)S(1)}, bf16[1024,128]{1,0:T(8,128)(2,1)}, u32[]{:S(2)}) copy-start(bf16[1024,128]{1,0:T(8,128)(2,1)} %amps.1) | copy-start | bytes 786436
  2.3 0.9 %copy-start.1 = (bf16[1,128,1024]{2,1,0:T(8,128)(2,1)S(1)}, bf16[1,128,1024]{2,1,0:T(8,128)(2,1)}, u32[]{:S(2)}) copy-start(bf16[1,128,1024]{2,1,0:T(8,128)(2,1)} %ints.1) | copy-start | bytes 786436
  3.3 0.7 %copy-start.4 = (s32[1,8]{1,0:T(1,128)S(1)}, s32[1,8]{1,0:T(1,128)}, u32[]{:S(2)}) copy-start(s32[1,8]{1,0:T(1,128)} %int_tiles.1) | copy-start | bytes 100
  34.7 0.7 %copy-start.2 = (s32[4]{0:T(128)S(1)}, s32[4]{0:T(128)}, u32[]{:S(2)}) copy-start(s32[4]{0:T(128)} %owners.1) | copy-start | bytes 52
  35.4 0.7 %copy-start.3 = (s32[8]{0:T(128)S(1)}, s32[8]{0:T(128)}, u32[]{:S(2)}) copy-start(s32[8]{0:T(128)} %ab_width.1) | copy-start | bytes 100

commit v2 on v1

v2 whole, which is shorter than its diff:
```python
import functools

import jax
import jax.numpy as jnp
from jax import lax
from jax.experimental import pallas as pl
from jax.experimental.pallas import tpu as pltpu
from jax.sharding import PartitionSpec as P

UP, DOWN, PAIR = 0, 1, 2


class Gather:
    def __init__(self, axis, count, own, slot_of, send_sem, recv_sem):
        me = lax.axis_index(axis)
        self.axis, self.half = axis, count // 2
        self.pos, self.side = me // 2, me % 2
        self.own, self.slot_of = own, slot_of
        self.send_sem, self.recv_sem = send_sem, recv_sem
        self.not_last = self.pos + 1 < self.half
        self.not_first = self.pos > 0
        self.up = {axis: jnp.minimum(self.pos + 1, self.half - 1) * 2 + self.side}
        self.down = {axis: jnp.maximum(self.pos - 1, 0) * 2 + self.side}
        self.pair = {axis: self.pos * 2 + 1 - self.side}

    def signal_all(self, barrier):
        def to(device):
            pl.semaphore_signal(
                barrier, inc=1, device_id=device, device_id_type=pl.DeviceIdType.MESH
            )

        to(self.pair)
        pl.when(self.not_last)(lambda: to(self.up))
        pl.when(self.not_first)(lambda: to(self.down))

    def neighbours(self):
        return 1 + self.not_last.astype(jnp.int32) + self.not_first.astype(jnp.int32)

    def copy(self, kind, p, src=None, side=None):
        slot = self.slot_of(p * 2 + (self.side if side is None else side))
        return pltpu.make_async_remote_copy(
            src_ref=slot if src is None else src,
            dst_ref=slot,
            send_sem=self.send_sem.at[kind, p],
            recv_sem=self.recv_sem.at[kind, p],
            device_id=(self.up, self.down, self.pair)[kind],
            device_id_type=pl.DeviceIdType.MESH,
        )

    def begin(self):
        pl.when(self.not_last)(lambda: self.copy(UP, self.pos, self.own).start())
        pl.when(self.not_first)(lambda: self.copy(DOWN, self.pos, self.own).start())
        self.copy(PAIR, self.pos, self.own).start()

    def steps(self, first, last):
        def step(s, carry):
            below, above = self.pos - 1 - s, self.pos + 1 + s

            @pl.when(below >= 0)
            def _():
                self.copy(UP, below).wait_recv()
                pl.when(self.not_last)(lambda: self.copy(UP, below).start())
                self.copy(PAIR, below).start()

            @pl.when(above < self.half)
            def _():
                self.copy(DOWN, above).wait_recv()
                pl.when(self.not_first)(lambda: self.copy(DOWN, above).start())
                self.copy(PAIR, above).start()

            return carry

        lax.fori_loop(first, last, step, 0)

    def finish(self):
        def one(p, carry):
            self.copy(PAIR, p, side=1 - self.side).wait_recv()
            self.copy(PAIR, p).wait_send()

            @pl.when(self.not_last & (p <= self.pos))
            def _():
                self.copy(UP, p).wait_send()

            @pl.when(self.not_first & (p >= self.pos))
            def _():
                self.copy(DOWN, p).wait_send()

            return carry

        lax.fori_loop(0, self.half, one, 0)


def ladder_kernel(
    groups, blocks, amps, amp_tiles, cd_width, ints, int_tiles, ab_width, owners, out,
    panels, all_amps, own_panel, own_amps, amp_tiles_s, cd_width_s, int_tiles_s, ab_width_s,
    owners_s, panel_send, panel_recv, amp_send, amp_recv, local, result, out_sem,
):
    rows, tile = own_amps.shape
    width = own_panel.shape[1]
    fetches = [
        pltpu.make_async_copy(source, target, local.at[i])
        for i, (source, target) in enumerate(
            (
                (int_tiles, int_tiles_s),
                (ints.at[0], own_panel),
                (amp_tiles, amp_tiles_s),
                (cd_width, cd_width_s),
                (amps, own_amps),
                (ab_width, ab_width_s),
                (owners, owners_s),
            )
        )
    ]
    for fetch in fetches:
        fetch.start()
    panel_gather = Gather(
        "grp", groups, own_panel, lambda i: panels.at[i], panel_send, panel_recv
    )
    amp_gather = Gather(
        "blk", blocks, own_amps,
        lambda i: all_amps.at[:, pl.ds(pl.multiple_of(i * tile, tile), tile)],
        amp_send, amp_recv,
    )
    barrier = pltpu.get_barrier_semaphore()
    panel_gather.signal_all(barrier)
    amp_gather.signal_all(barrier)

    fetches[0].wait()
    fetches[1].wait()
    for j in range(width // tile):
        cols = slice(j * tile, (j + 1) * tile)
        keep = jnp.full((tile, tile), int_tiles_s[0, j], jnp.int32) > 0
        own_panel[:, cols] = jnp.where(
            keep, own_panel[:, cols].astype(jnp.float32), 0.0
        ).astype(jnp.bfloat16)
    for fetch in fetches[2:5]:
        fetch.wait()
    within = lax.broadcasted_iota(jnp.int32, (tile, tile), 1) < cd_width_s[0]
    for r in range(rows // tile):
        part = slice(r * tile, (r + 1) * tile)
        keep = (jnp.full((tile, tile), amp_tiles_s[0, r], jnp.int32) > 0) & within
        own_amps[part, :] = jnp.where(keep, own_amps[part, :].astype(jnp.float32), 0.0).astype(
            jnp.bfloat16
        )
    pl.semaphore_wait(barrier, panel_gather.neighbours() + amp_gather.neighbours())
    panel_gather.begin()
    amp_gather.begin()

    panels[lax.axis_index("grp")] = own_panel[...]
    mine = pl.multiple_of(lax.axis_index("blk") * tile, tile)
    all_amps[:, pl.ds(mine, tile)] = own_amps[...]
    panel_gather.steps(0, 1)
    amp_gather.steps(0, blocks // 2 - 1)
    panel_gather.steps(1, groups // 2 - 1)
    amp_gather.finish()
    fetches[5].wait()
    fetches[6].wait()
    panel_gather.finish()

    column = lax.broadcasted_iota(jnp.int32, (rows, 2 * tile), 1)

    def store(j):
        cols = pl.ds(pl.multiple_of(j * 2 * tile, 2 * tile), 2 * tile)
        return pltpu.make_async_copy(result.at[:, cols], out.at[:, cols], out_sem.at[j])

    def columns(j, carry):
        cols = pl.ds(pl.multiple_of(j * 2 * tile, 2 * tile), 2 * tile)
        chosen = jnp.concatenate([panels[owners_s[t], :, cols] for t in range(blocks)], axis=0)
        total = jnp.dot(all_amps[...], chosen, preferred_element_type=jnp.float32)
        limit = jnp.where(column < tile, ab_width_s[2 * j], tile + ab_width_s[2 * j + 1])
        result[:, cols] = jnp.where(column < limit, 0.5 * total, 0.0).astype(out.dtype)
        store(j).start()
        return carry

    count = width // (2 * tile)
    lax.fori_loop(0, count, columns, 0)
    lax.fori_loop(0, count, lambda j, carry: (store(j).wait(), carry)[1], 0)


def per_device(amplitudes, amp_tiles, cd_width, integrals, int_tiles, ab_width, owners):
    rows, tile = amplitudes.shape
    width = integrals.shape[2]
    groups, blocks = lax.axis_size("grp"), lax.axis_size("blk")
    hbm = pl.BlockSpec(memory_space=pltpu.HBM)
    amp_tiles = amp_tiles.T
    return pl.pallas_call(
        functools.partial(ladder_kernel, groups, blocks),
        out_shape=jax.ShapeDtypeStruct((rows, width), jnp.bfloat16),
        in_specs=[hbm] * 7,
        out_specs=hbm,
        scratch_shapes=[
            pltpu.VMEM((groups, tile, width), jnp.bfloat16),
            pltpu.VMEM((rows, blocks * tile), jnp.bfloat16),
            pltpu.VMEM((tile, width), jnp.bfloat16),
            pltpu.VMEM((rows, tile), jnp.bfloat16),
            pltpu.SMEM(amp_tiles.shape, jnp.int32),
            pltpu.SMEM(cd_width.shape, jnp.int32),
            pltpu.SMEM(int_tiles.shape, jnp.int32),
            pltpu.SMEM(ab_width.shape, jnp.int32),
            pltpu.SMEM(owners.shape, jnp.int32),
            pltpu.SemaphoreType.DMA((3, groups // 2)),
            pltpu.SemaphoreType.DMA((3, groups // 2)),
            pltpu.SemaphoreType.DMA((3, blocks // 2)),
            pltpu.SemaphoreType.DMA((3, blocks // 2)),
            pltpu.SemaphoreType.DMA((7,)),
            pltpu.VMEM((rows, width), jnp.bfloat16),
            pltpu.SemaphoreType.DMA((width // (2 * tile),)),
        ],
        compiler_params=pltpu.CompilerParams(
            collective_id=0,
            has_side_effects=True,
            vmem_limit_bytes=60 * 2**20,
        ),
    )(amplitudes, amp_tiles, cd_width, integrals, int_tiles, ab_width, owners)


def solution(mesh):
    placed = (
        P("grp", "blk"),
        P("grp", "blk"),
        P("blk"),
        P("grp", None, "blk"),
        P("grp", "blk"),
        P("blk"),
        P(),
    )
    return jax.shard_map(
        per_device, mesh=mesh, in_specs=placed, out_specs=P("grp", "blk"), check_vma=False
    )
```

time: 39.9 us -> 36.8 us (0.922)
  local copies, waits for them, and re-layouts: 4.59 us -> 3.08 us
  Pallas kernels: 34.4 us -> 32.9 us
    unnamed x11 -> x1, local copies, waits for them, and re-layouts: 4.59 us -> 3.08 us
    pallas_call x2 -> x1, Pallas kernels: 34.4 us -> 32.9 us  [per_device(): pl.pallas_call(functools.partial(ladder_kernel, groups, blocks), out_shap...]
where the time goes in v2:
time: 36.8 us; the launch traced here: 36.7 us
  Pallas kernels  32.9 us (89%)
  local copies, waits for them, and re-layouts  3.08 us (8%)
  between operations  0.66 us (2%)
    pallas_call x1, Pallas kernels, per_device(): pl.pallas_call(functools.partial(ladder_kernel, groups, blocks), out_shap...  32.9 us
    unnamed x1, local copies, waits for them, and re-layouts  3.08 us

profile of v2, /device:TPU:0, one launch (start us, length us, event | category | flops | bytes accessed | tf_op | source)
XLA Modules:
  0.0 36.7 jit_solution(1617258783613490720)
XLA Ops:
  0.7 32.9 %shard_map.73 = bf16[1024,1024]{1,0:T(8,128)(2,1)} custom-call(bf16[1024,128]{1,0:T(8,128)(2,1)} %amps.1, s32[1,8]{1,0:T(1,128)} %bitcast.1, s32[1]{0:T(128)S(6)} %copy.9.cd_width, bf16[1,128,1024]{2,1,0:T(8,128)(2,1)} %ints.1, s32[1,8]{1,0:T(1,128)} %int_tiles.1, s32[8]{0:T(128)} %ab_width.1, s32[4]{0:T(128)} %owners.1), custom_call_target="tpu_custom_call" | custom-call | tf_op jit(solution)/shard_map/pallas_call | solution.py:186
  33.6 3.1 %copy.10 = bf16[1024,1024]{1,0:T(8,128)(2,1)} copy(bf16[1024,1024]{1,0:T(8,128)(2,1)} %shard_map.73) | data formatting | bytes 4194304

commit v3 on v2

v3 whole, which is shorter than its diff:
```python
import functools

import jax
import jax.numpy as jnp
from jax import lax
from jax.experimental import pallas as pl
from jax.experimental.pallas import tpu as pltpu
from jax.sharding import PartitionSpec as P

UP, DOWN, PAIR, CROSSED = 0, 1, 2, 3


class Gather:
    def __init__(self, axis, count, split, own, slot_of, send_sem, recv_sem):
        me = lax.axis_index(axis)
        self.half, self.split = count // 2, split
        self.pos, self.side = me // 2, me % 2
        self.own, self.slot_of = own, slot_of
        self.send_sem, self.recv_sem = send_sem, recv_sem
        self.not_last = self.pos + 1 < self.half
        self.not_first = self.pos > 0
        self.up = {axis: jnp.minimum(self.pos + 1, self.half - 1) * 2 + self.side}
        self.down = {axis: jnp.maximum(self.pos - 1, 0) * 2 + self.side}
        self.pair = {axis: self.pos * 2 + 1 - self.side}

    def signal_all(self, barrier):
        def to(device):
            pl.semaphore_signal(
                barrier, inc=1, device_id=device, device_id_type=pl.DeviceIdType.MESH
            )

        to(self.pair)
        pl.when(self.not_last)(lambda: to(self.up))
        pl.when(self.not_first)(lambda: to(self.down))

    def neighbours(self):
        return 1 + self.not_last.astype(jnp.int32) + self.not_first.astype(jnp.int32)

    def copy(self, kind, h, p, own=False, other=False):
        slot = self.slot_of(p * 2 + (1 - self.side if other else self.side), h)
        row = kind * 2 + h if kind < CROSSED else 2 * CROSSED + h
        target = (self.up, self.down, self.pair, (self.up, self.down)[h])[kind]
        if kind == CROSSED:
            slot = self.slot_of(p * 2 + 1 - self.side, 0)
        return pltpu.make_async_remote_copy(
            src_ref=self.own(h) if own else slot,
            dst_ref=slot,
            send_sem=self.send_sem.at[row, p],
            recv_sem=self.recv_sem.at[row, p],
            device_id=target,
            device_id_type=pl.DeviceIdType.MESH,
        )

    def cross(self, p):
        return self.split & ((p == 0) | (p == self.half - 1))

    def begin(self):
        for h in (0, 1):
            self.copy(PAIR, h, self.pos, own=True).start()
        for h in (1, 0):
            pl.when(self.not_last)(lambda h=h: self.copy(UP, h, self.pos, own=True).start())
            pl.when(self.not_first)(lambda h=h: self.copy(DOWN, h, self.pos, own=True).start())

    def begin_crossed(self):
        for way, end, last in ((UP, 0, self.half - 1), (DOWN, self.half - 1, 0)):

            @pl.when(self.pos == end)
            def _(way=way, end=end):
                self.copy(PAIR, 0, end, other=True).wait_recv()
                self.copy(CROSSED, way, end).start()

    def steps(self, first, last):
        def arrived(way, p, going_on, end):
            for h in (1, 0):
                self.copy(way, h, p).wait_recv()
                pl.when(going_on)(lambda h=h: self.copy(way, h, p).start())
                if h == 1 or not self.split:
                    self.copy(PAIR, h, p).start()
                else:
                    pl.when(jnp.logical_not(self.cross(p)))(
                        lambda h=h: self.copy(PAIR, h, p).start()
                    )
            if self.split:

                @pl.when(p == end)
                def _():
                    self.copy(CROSSED, way, end).wait_recv()
                    pl.when(going_on)(lambda: self.copy(CROSSED, way, end).start())

        def step(s, carry):
            below, above = self.pos - 1 - s, self.pos + 1 + s
            pl.when(below >= 0)(lambda: arrived(UP, below, self.not_last, 0))
            pl.when(above < self.half)(
                lambda: arrived(DOWN, above, self.not_first, self.half - 1)
            )
            return carry

        lax.fori_loop(first, last, step, 0)

    def finish(self):
        def one(p, carry):
            self.copy(PAIR, 1, p, other=True).wait_recv()
            self.copy(PAIR, 1, p).wait_send()
            if self.split:

                @pl.when(jnp.logical_not(self.cross(p)))
                def _():
                    self.copy(PAIR, 0, p, other=True).wait_recv()
                    self.copy(PAIR, 0, p).wait_send()

                @pl.when(self.cross(p) & (p == self.pos))
                def _():
                    self.copy(PAIR, 0, p).wait_send()

            else:
                self.copy(PAIR, 0, p, other=True).wait_recv()
                self.copy(PAIR, 0, p).wait_send()

            @pl.when(self.not_last & (p <= self.pos))
            def _():
                for h in (0, 1):
                    self.copy(UP, h, p).wait_send()

            @pl.when(self.not_first & (p >= self.pos))
            def _():
                for h in (0, 1):
                    self.copy(DOWN, h, p).wait_send()

            return carry

        lax.fori_loop(0, self.half, one, 0)
        if self.split:
            pl.when(self.not_last)(lambda: self.copy(CROSSED, UP, 0).wait_send())
            pl.when(self.not_first)(lambda: self.copy(CROSSED, DOWN, self.half - 1).wait_send())


def gather_kernel(
    groups, blocks, amps, amp_tiles, cd_width, ints, int_tiles, panels, all_amps,
    own_panel, own_amps, amp_tiles_s, cd_width_s, int_tiles_s,
    panel_send, panel_recv, amp_send, amp_recv, local,
):
    rows, tile = own_amps.shape
    width = own_panel.shape[1]
    fetches = [
        pltpu.make_async_copy(source, target, local.at[i])
        for i, (source, target) in enumerate(
            (
                (int_tiles, int_tiles_s),
                (ints.at[0], own_panel),
                (amp_tiles, amp_tiles_s),
                (cd_width, cd_width_s),
                (amps, own_amps),
            )
        )
    ]
    for fetch in fetches:
        fetch.start()
    panel_gather = Gather(
        "grp", groups, True,
        lambda h: own_panel.at[pl.ds(h * (tile // 2), tile // 2)],
        lambda i, h: panels.at[i, pl.ds(h * (tile // 2), tile // 2)],
        panel_send, panel_recv,
    )
    amp_gather = Gather(
        "blk", blocks, False,
        lambda h: own_amps.at[pl.ds(h * (rows // 2), rows // 2)],
        lambda i, h: all_amps.at[
            pl.ds(h * (rows // 2), rows // 2), pl.ds(pl.multiple_of(i * tile, tile), tile)
        ],
        amp_send, amp_recv,
    )
    barrier = pltpu.get_barrier_semaphore()
    panel_gather.signal_all(barrier)
    amp_gather.signal_all(barrier)

    fetches[0].wait()
    fetches[1].wait()
    for j in range(width // tile):
        cols = slice(j * tile, (j + 1) * tile)
        keep = jnp.full((tile, tile), int_tiles_s[0, j], jnp.int32) > 0
        own_panel[:, cols] = jnp.where(
            keep, own_panel[:, cols].astype(jnp.float32), 0.0
        ).astype(jnp.bfloat16)
    for fetch in fetches[2:]:
        fetch.wait()
    within = lax.broadcasted_iota(jnp.int32, (tile, tile), 1) < cd_width_s[0]
    for r in range(rows // tile):
        part = slice(r * tile, (r + 1) * tile)
        keep = (jnp.full((tile, tile), amp_tiles_s[0, r], jnp.int32) > 0) & within
        own_amps[part, :] = jnp.where(keep, own_amps[part, :].astype(jnp.float32), 0.0).astype(
            jnp.bfloat16
        )
    pl.semaphore_wait(barrier, panel_gather.neighbours() + amp_gather.neighbours())
    panel_gather.begin()
    amp_gather.begin()
    mine = pl.ds(pl.multiple_of(lax.axis_index("blk") * tile, tile), tile)
    keeps = [
        pltpu.make_async_copy(own_panel, panels.at[lax.axis_index("grp")], local.at[0]),
        pltpu.make_async_copy(own_amps, all_amps.at[:, mine], local.at[1]),
    ]
    for keep in keeps:
        keep.start()
    panel_gather.begin_crossed()
    panel_gather.steps(0, 1)
    amp_gather.steps(0, blocks // 2 - 1)
    panel_gather.steps(1, groups // 2 - 1)
    for keep in keeps:
        keep.wait()
    amp_gather.finish()
    panel_gather.finish()


def multiply_kernel(
    owners, ab_width, amps, panels, out, owners_s, ab_width_s, all_amps, chosen, result, sem, cut_sem, out_sem
):
    tile = panels.shape[1]
    rows, width = out.shape
    step = 2 * tile
    count = chosen.shape[0] // tile
    fetches = [
        pltpu.make_async_copy(source, target, sem.at[i])
        for i, (source, target) in enumerate(
            ((owners, owners_s), (ab_width, ab_width_s), (amps, all_amps))
        )
    ]
    for fetch in fetches:
        fetch.start()
    fetches[0].wait()
    pieces = [
        [
            pltpu.make_async_copy(
                panels.at[owners_s[t], :, pl.ds(j * step, step)],
                chosen.at[pl.ds(t * tile, tile), pl.ds(j * step, step)],
                cut_sem.at[j, t],
            )
            for t in range(count)
        ]
        for j in range(width // step)
    ]
    for cut in pieces:
        for piece in cut:
            piece.start()
    fetches[1].wait()
    fetches[2].wait()
    column = lax.broadcasted_iota(jnp.int32, (rows, step), 1)
    stores = []
    for j, cut in enumerate(pieces):
        for piece in cut:
            piece.wait()
        cols = slice(j * step, (j + 1) * step)
        total = jnp.dot(all_amps[...], chosen[:, cols], preferred_element_type=jnp.float32)
        limit = jnp.where(column < tile, ab_width_s[2 * j], tile + ab_width_s[2 * j + 1])
        result[:, cols] = jnp.where(column < limit, 0.5 * total, 0.0).astype(out.dtype)
        store = pltpu.make_async_copy(
            result.at[:, pl.ds(j * step, step)], out.at[:, pl.ds(j * step, step)], out_sem.at[j]
        )
        store.start()
        stores.append(store)
    for store in stores:
        store.wait()


def per_device(amplitudes, amp_tiles, cd_width, integrals, int_tiles, ab_width, owners):
    rows, tile = amplitudes.shape
    width = integrals.shape[2]
    groups, blocks = lax.axis_size("grp"), lax.axis_size("blk")
    hbm = pl.BlockSpec(memory_space=pltpu.HBM)
    amp_tiles = amp_tiles.T
    limit = 60 * 2**20
    panels, amps = pl.pallas_call(
        functools.partial(gather_kernel, groups, blocks),
        out_shape=(
            jax.ShapeDtypeStruct((groups, tile, width), jnp.bfloat16),
            jax.ShapeDtypeStruct((rows, blocks * tile), jnp.bfloat16),
        ),
        in_specs=[hbm] * 5,
        out_specs=(hbm, hbm),
        scratch_shapes=[
            pltpu.VMEM((tile, width), jnp.bfloat16),
            pltpu.VMEM((rows, tile), jnp.bfloat16),
            pltpu.SMEM(amp_tiles.shape, jnp.int32),
            pltpu.SMEM(cd_width.shape, jnp.int32),
            pltpu.SMEM(int_tiles.shape, jnp.int32),
            pltpu.SemaphoreType.DMA((8, groups // 2)),
            pltpu.SemaphoreType.DMA((8, groups // 2)),
            pltpu.SemaphoreType.DMA((8, blocks // 2)),
            pltpu.SemaphoreType.DMA((8, blocks // 2)),
            pltpu.SemaphoreType.DMA((5,)),
        ],
        compiler_params=pltpu.CompilerParams(
            collective_id=0, has_side_effects=True, vmem_limit_bytes=limit
        ),
    )(amplitudes, amp_tiles, cd_width, integrals, int_tiles)
    cuts = width // (2 * tile)
    return pl.pallas_call(
        multiply_kernel,
        out_shape=jax.ShapeDtypeStruct((rows, width), jnp.bfloat16),
        in_specs=[hbm] * 4,
        out_specs=hbm,
        scratch_shapes=[
            pltpu.SMEM(owners.shape, jnp.int32),
            pltpu.SMEM(ab_width.shape, jnp.int32),
            pltpu.VMEM((rows, blocks * tile), jnp.bfloat16),
            pltpu.VMEM((blocks * tile, width), jnp.bfloat16),
            pltpu.VMEM((rows, width), jnp.bfloat16),
            pltpu.SemaphoreType.DMA((3,)),
            pltpu.SemaphoreType.DMA((cuts, blocks)),
            pltpu.SemaphoreType.DMA((cuts,)),
        ],
        compiler_params=pltpu.CompilerParams(vmem_limit_bytes=limit),
    )(owners, ab_width, amps, panels)


def solution(mesh):
    placed = (
        P("grp", "blk"),
        P("grp", "blk"),
        P("blk"),
        P("grp", None, "blk"),
        P("grp", "blk"),
        P("blk"),
        P(),
    )
    return jax.shard_map(
        per_device, mesh=mesh, in_specs=placed, out_specs=P("grp", "blk"), check_vma=False
    )
```

time: 36.8 us -> 36.4 us (0.989)
  local copies, waits for them, and re-layouts: 3.08 us -> 0 us
  Pallas kernels: 32.9 us -> 35.5 us
    unnamed x1 -> x0, local copies, waits for them, and re-layouts: 3.08 us -> none
    pallas_call x1 -> x2, Pallas kernels: 32.9 us -> 35.5 us  [the longest x1 30.1 us: per_device(): pl.pallas_call(functools.partial(gather_kernel, groups, blocks), out_shap...]
where the time goes in v3:
time: 36.4 us; the launch traced here: 36.2 us
  Pallas kernels  35.5 us (98%)
  between operations  0.66 us (2%)
    pallas_call x1, Pallas kernels, per_device(): pl.pallas_call(functools.partial(gather_kernel, groups, blocks), out_shap...  30.1 us
    pallas_call x1, Pallas kernels, per_device(): pl.pallas_call(multiply_kernel, out_shape=jax.ShapeDtypeStruct((rows, wid...  5.44 us

profile of v3, /device:TPU:0, one launch (start us, length us, event | category | flops | bytes accessed | tf_op | source)
XLA Modules:
  0.0 36.2 jit_solution(17267713031419350348)
XLA Ops:
  0.7 30.1 %shard_map.73 = (bf16[8,128,1024]{2,1,0:T(8,128)(2,1)}, bf16[1024,512]{1,0:T(8,128)(2,1)}) custom-call(bf16[1024,128]{1,0:T(8,128)(2,1)} %amps.1, s32[1,8]{1,0:T(1,128)} %bitcast.1, s32[1]{0:T(128)S(6)} %copy.8.cd_width, bf16[1,128,1024]{2,1,0:T(8,128)(2,1)} %ints.1, s32[1,8]{1,0:T(1,128)} %int_tiles.1), custom_call_target="tpu_custom_call" | custom-call | tf_op jit(solution)/shard_map/pallas_call | solution.py:270
  30.7 5.4 %shard_map.74 = bf16[1024,1024]{1,0:T(8,128)(2,1)} custom-call(s32[4]{0:T(128)} %owners.1, s32[8]{0:T(128)} %ab_width.1, bf16[1024,512]{1,0:T(8,128)(2,1)} %get-tuple-element.7.amps, bf16[8,128,1024]{2,1,0:T(8,128)(2,1)} %get-tuple-element.8.panels), custom_call_target="tpu_custom_call" | custom-call | tf_op jit(solution)/shard_map/pallas_call | solution.py:295

commit v4 on v3

--- a/solution.py
+++ b/solution.py
@@ -181,6 +181,8 @@
         own_panel[:, cols] = jnp.where(
             keep, own_panel[:, cols].astype(jnp.float32), 0.0
         ).astype(jnp.bfloat16)
+    pl.semaphore_wait(barrier, panel_gather.neighbours() + amp_gather.neighbours())
+    panel_gather.begin()
     for fetch in fetches[2:]:
         fetch.wait()
     within = lax.broadcasted_iota(jnp.int32, (tile, tile), 1) < cd_width_s[0]
@@ -190,8 +192,6 @@
         own_amps[part, :] = jnp.where(keep, own_amps[part, :].astype(jnp.float32), 0.0).astype(
             jnp.bfloat16
         )
-    pl.semaphore_wait(barrier, panel_gather.neighbours() + amp_gather.neighbours())
-    panel_gather.begin()
     amp_gather.begin()
     mine = pl.ds(pl.multiple_of(lax.axis_index("blk") * tile, tile), tile)
     keeps = [
@@ -211,53 +211,69 @@
 
 
 def multiply_kernel(
-    owners, ab_width, amps, panels, out, owners_s, ab_width_s, all_amps, chosen, result, sem, cut_sem, out_sem
+    owners, ab_width, amps, panels, out,
+    owners_s, ab_width_s, all_amps, held, result, sem, held_sem, amp_sem, out_sem,
 ):
     tile = panels.shape[1]
     rows, width = out.shape
-    step = 2 * tile
-    count = chosen.shape[0] // tile
+    count = owners.shape[0]
+    part = rows // amp_sem.shape[0]
+    whole = held.shape[0] == panels.shape[0]
+
+    def rows_of(r):
+        return pl.ds(pl.multiple_of(r * part, part), part)
+
+    def fetch_amps(r):
+        return pltpu.make_async_copy(
+            amps.at[rows_of(r)], all_amps.at[rows_of(r)], amp_sem.at[r]
+        )
+
+    def store(r):
+        return pltpu.make_async_copy(result.at[rows_of(r)], out.at[rows_of(r)], out_sem.at[r])
+
+    scalars = [
+        pltpu.make_async_copy(owners, owners_s, sem.at[0]),
+        pltpu.make_async_copy(ab_width, ab_width_s, sem.at[1]),
+    ]
+    for fetch in scalars:
+        fetch.start()
+    if not whole:
+        scalars[0].wait()
     fetches = [
-        pltpu.make_async_copy(source, target, sem.at[i])
-        for i, (source, target) in enumerate(
-            ((owners, owners_s), (ab_width, ab_width_s), (amps, all_amps))
-        )
+        pltpu.make_async_copy(panels.at[i if whole else owners_s[i]], held.at[i], held_sem.at[i])
+        for i in range(held.shape[0])
     ]
     for fetch in fetches:
         fetch.start()
-    fetches[0].wait()
-    pieces = [
-        [
-            pltpu.make_async_copy(
-                panels.at[owners_s[t], :, pl.ds(j * step, step)],
-                chosen.at[pl.ds(t * tile, tile), pl.ds(j * step, step)],
-                cut_sem.at[j, t],
-            )
-            for t in range(count)
-        ]
-        for j in range(width // step)
-    ]
-    for cut in pieces:
-        for piece in cut:
-            piece.start()
-    fetches[1].wait()
-    fetches[2].wait()
-    column = lax.broadcasted_iota(jnp.int32, (rows, step), 1)
-    stores = []
-    for j, cut in enumerate(pieces):
-        for piece in cut:
-            piece.wait()
-        cols = slice(j * step, (j + 1) * step)
-        total = jnp.dot(all_amps[...], chosen[:, cols], preferred_element_type=jnp.float32)
-        limit = jnp.where(column < tile, ab_width_s[2 * j], tile + ab_width_s[2 * j + 1])
-        result[:, cols] = jnp.where(column < limit, 0.5 * total, 0.0).astype(out.dtype)
-        store = pltpu.make_async_copy(
-            result.at[:, pl.ds(j * step, step)], out.at[:, pl.ds(j * step, step)], out_sem.at[j]
-        )
-        store.start()
-        stores.append(store)
-    for store in stores:
-        store.wait()
+    for r in range(rows // part):
+        fetch_amps(r).start()
+    if whole:
+        scalars[0].wait()
+    scalars[1].wait()
+    for fetch in fetches:
+        fetch.wait()
+    column = lax.broadcasted_iota(jnp.int32, (1, 2 * tile), 1)
+
+    def multiply(r, carry):
+        fetch_amps(r).wait()
+        for j in range(0, width // tile, 2):
+            cols = slice(j * tile, (j + 2) * tile)
+            chosen = jnp.concatenate(
+                [held[owners_s[t] if whole else t, :, cols] for t in range(count)], axis=0
+            )
+            total = jnp.dot(
+                all_amps[rows_of(r), :], chosen, preferred_element_type=jnp.float32
+            )
+            limit = jnp.where(column < tile, ab_width_s[j], tile + ab_width_s[j + 1])
+            result[rows_of(r), cols] = jnp.where(column < limit, 0.5 * total, 0.0).astype(
+                out.dtype
+            )
+        store(r).start()
+        return carry
+
+    parts = rows // part
+    lax.fori_loop(0, parts, multiply, 0)
+    lax.fori_loop(0, parts, lambda r, carry: (store(r).wait(), carry)[1], 0)
 
 
 def per_device(amplitudes, amp_tiles, cd_width, integrals, int_tiles, ab_width, owners):
@@ -291,7 +307,7 @@
             collective_id=0, has_side_effects=True, vmem_limit_bytes=limit
         ),
     )(amplitudes, amp_tiles, cd_width, integrals, int_tiles)
-    cuts = width // (2 * tile)
+    held = groups if groups <= 2 * blocks else blocks
     return pl.pallas_call(
         multiply_kernel,
         out_shape=jax.ShapeDtypeStruct((rows, width), jnp.bfloat16),
@@ -301,11 +317,12 @@
             pltpu.SMEM(owners.shape, jnp.int32),
             pltpu.SMEM(ab_width.shape, jnp.int32),
             pltpu.VMEM((rows, blocks * tile), jnp.bfloat16),
-            pltpu.VMEM((blocks * tile, width), jnp.bfloat16),
+            pltpu.VMEM((held, tile, width), jnp.bfloat16),
             pltpu.VMEM((rows, width), jnp.bfloat16),
-            pltpu.SemaphoreType.DMA((3,)),
-            pltpu.SemaphoreType.DMA((cuts, blocks)),
-            pltpu.SemaphoreType.DMA((cuts,)),
+            pltpu.SemaphoreType.DMA((2,)),
+            pltpu.SemaphoreType.DMA((held,)),
+            pltpu.SemaphoreType.DMA((2,)),
+            pltpu.SemaphoreType.DMA((2,)),
         ],
         compiler_params=pltpu.CompilerParams(vmem_limit_bytes=limit),
     )(owners, ab_width, amps, panels)

time: 36.4 us -> 35.1 us (0.964)
  Pallas kernels: 35.5 us -> 34.3 us
    pallas_call x1, Pallas kernels: 5.44 us -> 4.19 us  [per_device(): pl.pallas_call(multiply_kernel, out_shape=jax.ShapeDtypeStruct((rows, wid...]
where the time goes in v4:
time: 35.1 us; the launch traced here: 34.9 us
  Pallas kernels  34.3 us (98%)
  between operations  0.66 us (2%)
    pallas_call x1, Pallas kernels, per_device(): pl.pallas_call(functools.partial(gather_kernel, groups, blocks), out_shap...  30.1 us
    pallas_call x1, Pallas kernels, per_device(): pl.pallas_call(multiply_kernel, out_shape=jax.ShapeDtypeStruct((rows, wid...  4.19 us

profile of v4, /device:TPU:0, one launch (start us, length us, event | category | flops | bytes accessed | tf_op | source)
XLA Modules:
  0.0 34.9 jit_solution(2588930098353016580)
XLA Ops:
  0.7 30.1 %shard_map.73 = (bf16[8,128,1024]{2,1,0:T(8,128)(2,1)}, bf16[1024,512]{1,0:T(8,128)(2,1)}) custom-call(bf16[1024,128]{1,0:T(8,128)(2,1)} %amps.1, s32[1,8]{1,0:T(1,128)} %bitcast.1, s32[1]{0:T(128)S(6)} %copy.8.cd_width, bf16[1,128,1024]{2,1,0:T(8,128)(2,1)} %ints.1, s32[1,8]{1,0:T(1,128)} %int_tiles.1), custom_call_target="tpu_custom_call" | custom-call | tf_op jit(solution)/shard_map/pallas_call | solution.py:286
  30.7 4.2 %shard_map.74 = bf16[1024,1024]{1,0:T(8,128)(2,1)} custom-call(s32[4]{0:T(128)} %owners.1, s32[8]{0:T(128)} %ab_width.1, bf16[1024,512]{1,0:T(8,128)(2,1)} %get-tuple-element.7.amps, bf16[8,128,1024]{2,1,0:T(8,128)(2,1)} %get-tuple-element.8.panels), custom_call_target="tpu_custom_call" | custom-call | tf_op jit(solution)/shard_map/pallas_call | solution.py:311

commit v5 on v4

--- a/solution.py
+++ b/solution.py
@@ -70,29 +70,27 @@
                 self.copy(CROSSED, way, end).start()
 
     def steps(self, first, last):
-        def arrived(way, p, going_on, end):
-            for h in (1, 0):
-                self.copy(way, h, p).wait_recv()
-                pl.when(going_on)(lambda h=h: self.copy(way, h, p).start())
-                if h == 1 or not self.split:
-                    self.copy(PAIR, h, p).start()
-                else:
-                    pl.when(jnp.logical_not(self.cross(p)))(
-                        lambda h=h: self.copy(PAIR, h, p).start()
-                    )
-            if self.split:
-
-                @pl.when(p == end)
-                def _():
-                    self.copy(CROSSED, way, end).wait_recv()
-                    pl.when(going_on)(lambda: self.copy(CROSSED, way, end).start())
+        def arrived(way, h, p, going_on):
+            self.copy(way, h, p).wait_recv()
+            pl.when(going_on)(lambda: self.copy(way, h, p).start())
+            if h == 1 or not self.split:
+                self.copy(PAIR, h, p).start()
+            else:
+                pl.when(jnp.logical_not(self.cross(p)))(lambda: self.copy(PAIR, h, p).start())
+
+        def crossed(way, p, going_on):
+            self.copy(CROSSED, way, p).wait_recv()
+            pl.when(going_on)(lambda: self.copy(CROSSED, way, p).start())
 
         def step(s, carry):
             below, above = self.pos - 1 - s, self.pos + 1 + s
-            pl.when(below >= 0)(lambda: arrived(UP, below, self.not_last, 0))
-            pl.when(above < self.half)(
-                lambda: arrived(DOWN, above, self.not_first, self.half - 1)
-            )
+            for h in (1, 0):
+                pl.when(below >= 0)(lambda h=h: arrived(UP, h, below, self.not_last))
+                pl.when(above < self.half)(lambda h=h: arrived(DOWN, h, above, self.not_first))
+            if self.split:
+                end = self.half - 1
+                pl.when(below == 0)(lambda: crossed(UP, 0, self.not_last))
+                pl.when(above == end)(lambda: crossed(DOWN, end, self.not_first))
             return carry
 
         lax.fori_loop(first, last, step, 0)

time: 35.1 us -> 31.6 us (0.900)
  Pallas kernels: 34.3 us -> 30.8 us
    pallas_call x1, Pallas kernels: 30.1 us -> 26.6 us  [per_device(): pl.pallas_call(functools.partial(gather_kernel, groups, blocks), out_shap...]
where the time goes in v5:
time: 31.6 us; the launch traced here: 31.5 us
  Pallas kernels  30.8 us (97%)
  between operations  0.66 us (2%)
    pallas_call x1, Pallas kernels, per_device(): pl.pallas_call(functools.partial(gather_kernel, groups, blocks), out_shap...  26.6 us
    pallas_call x1, Pallas kernels, per_device(): pl.pallas_call(multiply_kernel, out_shape=jax.ShapeDtypeStruct((rows, wid...  4.19 us

profile of v5, /device:TPU:0, one launch (start us, length us, event | category | flops | bytes accessed | tf_op | source)
XLA Modules:
  0.0 31.5 jit_solution(15023048072263931150)
XLA Ops:
  0.7 26.6 %shard_map.73 = (bf16[8,128,1024]{2,1,0:T(8,128)(2,1)}, bf16[1024,512]{1,0:T(8,128)(2,1)}) custom-call(bf16[1024,128]{1,0:T(8,128)(2,1)} %amps.1, s32[1,8]{1,0:T(1,128)} %bitcast.1, s32[1]{0:T(128)S(6)} %copy.8.cd_width, bf16[1,128,1024]{2,1,0:T(8,128)(2,1)} %ints.1, s32[1,8]{1,0:T(1,128)} %int_tiles.1), custom_call_target="tpu_custom_call" | custom-call | tf_op jit(solution)/shard_map/pallas_call | solution.py:284
  27.3 4.2 %shard_map.74 = bf16[1024,1024]{1,0:T(8,128)(2,1)} custom-call(s32[4]{0:T(128)} %owners.1, s32[8]{0:T(128)} %ab_width.1, bf16[1024,512]{1,0:T(8,128)(2,1)} %get-tuple-element.7.amps, bf16[8,128,1024]{2,1,0:T(8,128)(2,1)} %get-tuple-element.8.panels), custom_call_target="tpu_custom_call" | custom-call | tf_op jit(solution)/shard_map/pallas_call | solution.py:309

commit v6 on v5

--- a/solution.py
+++ b/solution.py
@@ -226,9 +226,6 @@
             amps.at[rows_of(r)], all_amps.at[rows_of(r)], amp_sem.at[r]
         )
 
-    def store(r):
-        return pltpu.make_async_copy(result.at[rows_of(r)], out.at[rows_of(r)], out_sem.at[r])
-
     scalars = [
         pltpu.make_async_copy(owners, owners_s, sem.at[0]),
         pltpu.make_async_copy(ab_width, ab_width_s, sem.at[1]),
@@ -237,41 +234,44 @@
         fetch.start()
     if not whole:
         scalars[0].wait()
-    fetches = [
-        pltpu.make_async_copy(panels.at[i if whole else owners_s[i]], held.at[i], held_sem.at[i])
-        for i in range(held.shape[0])
-    ]
-    for fetch in fetches:
-        fetch.start()
+    parts = held_sem.shape[0]
+    span = width // parts
+
+    def fetch_panel(c, i):
+        cols = pl.ds(c * span, span)
+        return pltpu.make_async_copy(
+            panels.at[i if whole else owners_s[i], :, cols], held.at[i, :, cols], held_sem.at[c, i]
+        )
+
+    def store(c):
+        cols = pl.ds(c * span, span)
+        return pltpu.make_async_copy(result.at[:, cols], out.at[:, cols], out_sem.at[c])
+
     for r in range(rows // part):
         fetch_amps(r).start()
+    for c in range(parts):
+        for i in range(held.shape[0]):
+            fetch_panel(c, i).start()
     if whole:
         scalars[0].wait()
     scalars[1].wait()
-    for fetch in fetches:
-        fetch.wait()
+    for r in range(rows // part):
+        fetch_amps(r).wait()
     column = lax.broadcasted_iota(jnp.int32, (1, 2 * tile), 1)
-
-    def multiply(r, carry):
-        fetch_amps(r).wait()
-        for j in range(0, width // tile, 2):
+    for c in range(parts):
+        for i in range(held.shape[0]):
+            fetch_panel(c, i).wait()
+        for j in range(c * span // tile, (c + 1) * span // tile, 2):
             cols = slice(j * tile, (j + 2) * tile)
             chosen = jnp.concatenate(
                 [held[owners_s[t] if whole else t, :, cols] for t in range(count)], axis=0
             )
-            total = jnp.dot(
-                all_amps[rows_of(r), :], chosen, preferred_element_type=jnp.float32
-            )
+            total = jnp.dot(all_amps[...], chosen, preferred_element_type=jnp.float32)
             limit = jnp.where(column < tile, ab_width_s[j], tile + ab_width_s[j + 1])
-            result[rows_of(r), cols] = jnp.where(column < limit, 0.5 * total, 0.0).astype(
-                out.dtype
-            )
-        store(r).start()
-        return carry
-
-    parts = rows // part
-    lax.fori_loop(0, parts, multiply, 0)
-    lax.fori_loop(0, parts, lambda r, carry: (store(r).wait(), carry)[1], 0)
+            result[:, cols] = jnp.where(column < limit, 0.5 * total, 0.0).astype(out.dtype)
+        store(c).start()
+    for c in range(parts):
+        store(c).wait()
 
 
 def per_device(amplitudes, amp_tiles, cd_width, integrals, int_tiles, ab_width, owners):
@@ -318,7 +318,7 @@
             pltpu.VMEM((held, tile, width), jnp.bfloat16),
             pltpu.VMEM((rows, width), jnp.bfloat16),
             pltpu.SemaphoreType.DMA((2,)),
-            pltpu.SemaphoreType.DMA((held,)),
+            pltpu.SemaphoreType.DMA((2, held)),
             pltpu.SemaphoreType.DMA((2,)),
             pltpu.SemaphoreType.DMA((2,)),
         ],

time: 31.6 us -> 32 us (1.013)
  no operation moved by 1% of the time
where the time goes in v6:
time: 32 us; the launch traced here: 31.8 us
  Pallas kernels  31.1 us (97%)
  between operations  0.66 us (2%)
    pallas_call x1, Pallas kernels, per_device(): pl.pallas_call(functools.partial(gather_kernel, groups, blocks), out_shap...  26.6 us
    pallas_call x1, Pallas kernels, per_device(): pl.pallas_call(multiply_kernel, out_shape=jax.ShapeDtypeStruct((rows, wid...  4.51 us

profile of v6, /device:TPU:0, one launch (start us, length us, event | category | flops | bytes accessed | tf_op | source)
XLA Modules:
  0.0 31.8 jit_solution(8464122497690255753)
XLA Ops:
  0.7 26.6 %shard_map.73 = (bf16[8,128,1024]{2,1,0:T(8,128)(2,1)}, bf16[1024,512]{1,0:T(8,128)(2,1)}) custom-call(bf16[1024,128]{1,0:T(8,128)(2,1)} %amps.1, s32[1,8]{1,0:T(1,128)} %bitcast.1, s32[1]{0:T(128)S(6)} %copy.8.cd_width, bf16[1,128,1024]{2,1,0:T(8,128)(2,1)} %ints.1, s32[1,8]{1,0:T(1,128)} %int_tiles.1), custom_call_target="tpu_custom_call" | custom-call | tf_op jit(solution)/shard_map/pallas_call | solution.py:284
  27.3 4.5 %shard_map.74 = bf16[1024,1024]{1,0:T(8,128)(2,1)} custom-call(s32[4]{0:T(128)} %owners.1, s32[8]{0:T(128)} %ab_width.1, bf16[1024,512]{1,0:T(8,128)(2,1)} %get-tuple-element.7.amps, bf16[8,128,1024]{2,1,0:T(8,128)(2,1)} %get-tuple-element.8.panels), custom_call_target="tpu_custom_call" | custom-call | tf_op jit(solution)/shard_map/pallas_call | solution.py:309
